TPU v7x, 256 devices: a whole 4x4x8 slice. The times are simulated.
256 devices in a mesh: frame: 32 (over x, y, core), head: 8 (over z).
Axes of the slice: x: 4, y: 4, z: 8, core: 2. Of those that a mesh axis runs over, the one named last changes fastest.
Arguments:
- queries: bfloat16 [7168, 3072], P('frame', 'head'), may hold values from -24 to 24
- key_rows: bfloat16 [7168, 3072], P('frame', 'head'), may hold values from -24 to 24
- value_rows: bfloat16 [7168, 3072], P('frame', 'head'), may hold values from -5 to 5
- ref_keys: bfloat16 [32, 1024, 3072], P('frame', None, 'head'), may hold values from -5 to 5
- ref_values: bfloat16 [32, 1024, 3072], P('frame', None, 'head'), may hold values from -5 to 5
- key_lists: int32 [32, 8], P('frame'), may hold values from 0 to 31, as said below
- list_counts: int32 [32], P('frame'), may hold values from 1 to 8, as said below
- owner_index: int32 [1], replicated, may hold values from 0 to 31
- out_weight: bfloat16 [3072, 3072], P('head'), may hold values from -1.5 to 1.5
- residual: bfloat16 [7168, 3072], P('frame', 'head'), may hold values from -3 to 3
- gate_scale: float32 [3072], P('head'), may hold values from 0.5 to 2
Outputs:
- block_out: bfloat16 [7168, 3072], P('frame', 'head')
Inputs may be any that keep to these rules, and one draw needn't show every extreme that they name: `key_lists`: the first list_counts[f] entries of row f are distinct frames other than f, each within 4 frames of f; the remaining entries equal f. `list_counts`: some frame lists every frame within 4 of it.
All inputs are finite; a program needn't handle non-finite values.
Results may differ from a plain program's by a relative error of at most 0.02.
Values may be sent and summed in bfloat16 or wider, within the bound.
A program may use at most 64 MiB of HBM per device.

v0:
```python
import math
import jax
import jax.numpy as jnp
from jax import lax
from jax.sharding import PartitionSpec as P

HD = 128
REACH = 4


def broadcast(block, axis, source):
    block = jnp.where(lax.axis_index(axis) == source, block, jnp.zeros_like(block))
    return lax.psum(block, axis)


def from_behind(block, axis, distance):
    devices = range(lax.axis_size(axis))
    route = [(i - distance, i) for i in devices if i - distance in devices]
    return lax.ppermute(block, axis, route)


def absorb(carried, query_heads, key_block, value_block, allowed):
    running_max, running_sum, weighted = carried
    head_count = query_heads.shape[1]
    key_heads = key_block.reshape(key_block.shape[0], head_count, HD)
    value_heads = value_block.reshape(value_block.shape[0], head_count, HD)
    scores = jnp.einsum(
        "qhd,khd->hqk", query_heads, key_heads, preferred_element_type=jnp.float32
    ) * (1.0 / math.sqrt(HD))
    if allowed is not None:
        scores = jnp.where(allowed[None, None, :], scores, -jnp.inf)
    new_max = jnp.maximum(running_max, jnp.max(scores, axis=-1))
    factor = jnp.exp(running_max - new_max)
    weights = jnp.exp(scores - new_max[:, :, None])
    running_sum = running_sum * factor + jnp.sum(weights, axis=-1)
    weighted = weighted * factor.T[:, :, None] + jnp.einsum(
        "hqk,khd->qhd",
        weights.astype(jnp.bfloat16),
        value_heads,
        preferred_element_type=jnp.float32,
    )
    return (new_max, running_sum, weighted)


def frame_block(carried, query_heads, key_block, value_block, begin_row, listed, live_slots):
    frame_of = (begin_row + jnp.arange(key_block.shape[0], dtype=jnp.int32)) // query_heads.shape[0]
    allowed = jnp.any((frame_of[:, None] == listed[None, :]) & live_slots[None, :], axis=1)
    return lax.cond(
        jnp.any(allowed),
        lambda current: absorb(current, query_heads, key_block, value_block, allowed),
        lambda current: current,
        carried,
    )


def per_device(
    queries,
    key_rows,
    value_rows,
    ref_keys,
    ref_values,
    key_lists,
    list_counts,
    owner_index,
    out_weight,
    residual,
    gate_scale,
):
    frame_len = queries.shape[0]
    columns_here = queries.shape[1]
    head_count = columns_here // HD
    query_heads = queries.reshape(frame_len, head_count, HD)
    listed = key_lists[0]
    live_slots = jnp.arange(listed.shape[0], dtype=jnp.int32) < list_counts[0]
    position = lax.axis_index("frame")
    carried = (
        jnp.full((head_count, frame_len), -jnp.inf, jnp.float32),
        jnp.zeros((head_count, frame_len), jnp.float32),
        jnp.zeros((frame_len, head_count, HD), jnp.float32),
    )
    style_keys, style_values = (
        broadcast(ref_keys, "frame", owner_index[0]),
        broadcast(ref_values, "frame", owner_index[0]),
    )
    carried = absorb(carried, query_heads, style_keys[0], style_values[0], None)
    carried = absorb(carried, query_heads, key_rows, value_rows, None)
    for offset in list(range(1, REACH + 1)) + list(range(-REACH, 0)):
        moved_keys, moved_values = from_behind((key_rows, value_rows), "frame", offset)
        carried = frame_block(
            carried,
            query_heads,
            moved_keys,
            moved_values,
            (position - offset) * frame_len,
            listed,
            live_slots,
        )
    running_max, running_sum, weighted = carried
    attended = (
        (weighted / running_sum.T[:, :, None]).astype(jnp.bfloat16).reshape(frame_len, columns_here)
    )
    shares = lax.psum_scatter(
        lax.dot_general(
            out_weight, attended, (((0,), (1,)), ((), ())), preferred_element_type=jnp.float32
        ).astype(jnp.bfloat16),
        "head",
        scatter_dimension=0,
        tiled=True,
    ).astype(jnp.float32)
    return (residual.astype(jnp.float32) + gate_scale[None, :] * shares.T).astype(jnp.bfloat16)


def solution(mesh):
    placed = (
        P("frame", "head"),
        P("frame", "head"),
        P("frame", "head"),
        P("frame", None, "head"),
        P("frame", None, "head"),
        P("frame", None),
        P("frame"),
        P(),
        P("head", None),
        P("frame", "head"),
        P("head"),
    )
    return jax.shard_map(
        per_device, mesh=mesh, in_specs=placed, out_specs=P("frame", "head"), check_vma=False
    )
```

profile of v0, /device:TPU:2, one launch (start us, length us, event | category | flops | bytes accessed | tf_op | source)
XLA Modules:
  0.0 269.7 jit_solution(7305506349866342035)
XLA Ops:
  6.5 1.9 copy.128
  8.4 1.9 collective-permute-start
  10.3 3.5 %collective-permute-start.2 = (bf16[224,384]{0,1:T(8,128)(2,1)}, bf16[224,384]{0,1:T(8,128)(2,1)}, u32[]{:S(2)}, u32[]{:S(2)}) collective-permute-start(bf16[224,384]{0,1:T(8,128)(2,1)} %copy.128), channel_id=1, source_target_pairs={{0,16},{8,24},{16,32},{24,40},{32,48},{40,56},{48,64},{56,72},{64,... | collective-permute-start | bytes 516104 | tf_op jit(solution)/shard_map/ppermute | solution.py:19
  13.8 1.1 copy.133
  14.9 3.3 %collective-permute-start.1 = (bf16[224,384]{0,1:T(8,128)(2,1)S(1)}, bf16[224,384]{0,1:T(8,128)(2,1)}, u32[]{:S(2)}, u32[]{:S(2)}) collective-permute-start(bf16[224,384]{0,1:T(8,128)(2,1)S(1)} %copy.133), channel_id=1, source_target_pairs={{0,8},{8,16},{16,24},{24,32},{32,40},{40,48},{48,56},{56,64},{64,7... | collective-permute-start | bytes 516104 | tf_op jit(solution)/shard_map/ppermute | solution.py:19
  18.2 3.2 %collective-permute-start.3 = (bf16[224,384]{0,1:T(8,128)(2,1)S(1)}, bf16[224,384]{0,1:T(8,128)(2,1)}, u32[]{:S(2)}, u32[]{:S(2)}) collective-permute-start(bf16[224,384]{0,1:T(8,128)(2,1)S(1)} %copy.133), channel_id=1, source_target_pairs={{0,16},{8,24},{16,32},{24,40},{32,48},{40,56},{48,64},{56,72},{64,... | collective-permute-start | bytes 516104 | tf_op jit(solution)/shard_map/ppermute | solution.py:19
  21.4 2.7 collective-permute-start.4
  24.7 2.3 copy.124
  27.0 1.2 copy.131
  28.2 1.0 broadcast_select_fusion
  29.2 2.3 copy.125
  31.5 1.2 copy.132
  32.8 1.1 copy.126
  34.6 1.5 fusion.89
  41.0 2.1 fusion.105
  43.1 108.5 %all-reduce.3.cloned.1.call-done = (bf16[1024,3,128]{2,0,1:T(8,128)(2,1)}, bf16[1024,3,128]{2,0,1:T(8,128)(2,1)}) async-done(((bf16[1024,3,128]{2,0,1:T(8,128)(2,1)}, bf16[1024,3,128]{2,0,1:T(8,128)(2,1)}), (bf16[1024,3,128]{2,0,1:T(8,128)(2,1)}, bf16[1024,3,128]{2,0,1:T(8,128)(2,1)})) %all-reduce.3.cloned.1.call-update) | async-done | bytes 1572880 | tf_op jit(solution)/shard_map/psum | solution.py:13
  151.6 1.9 bitcast_reduce_fusion
  153.5 1.0 fusion.71
  154.5 1.9 collective-permute-start.5
  156.4 0.3 fusion.64
  156.8 5.5 %collective-permute-start.6 = (bf16[224,384]{0,1:T(8,128)(2,1)}, bf16[224,384]{0,1:T(8,128)(2,1)S(1)}, u32[]{:S(2)}, u32[]{:S(2)}) collective-permute-start(bf16[224,384]{0,1:T(8,128)(2,1)} %copy.128), channel_id=1, source_target_pairs={{0,32},{8,40},{16,48},{24,56},{32,64},{40,72},{48,80},{56,88},{64,... | collective-permute-start | bytes 516104 | tf_op jit(solution)/shard_map/ppermute | solution.py:19
  162.3 2.8 %collective-permute-start.7 = (bf16[224,384]{0,1:T(8,128)(2,1)S(1)}, bf16[224,384]{0,1:T(8,128)(2,1)S(1)}, u32[]{:S(2)}, u32[]{:S(2)}) collective-permute-start(bf16[224,384]{0,1:T(8,128)(2,1)S(1)} %copy.133), channel_id=1, source_target_pairs={{0,32},{8,40},{16,48},{24,56},{32,64},{40,72},{48,80},{56,88},{64,... | collective-permute-start | bytes 516104 | tf_op jit(solution)/shard_map/ppermute | solution.py:19
  165.1 5.5 %collective-permute-start.8 = (bf16[224,384]{0,1:T(8,128)(2,1)}, bf16[224,384]{0,1:T(8,128)(2,1)S(1)}, u32[]{:S(2)}, u32[]{:S(2)}) collective-permute-start(bf16[224,384]{0,1:T(8,128)(2,1)} %copy.128), channel_id=1, source_target_pairs={{32,0},{40,8},{48,16},{56,24},{64,32},{72,40},{80,48},{88,56},{96,... | collective-permute-start | bytes 516104 | tf_op jit(solution)/shard_map/ppermute | solution.py:19
  170.6 1.9 collective-permute-start.9
  172.5 0.7 copy-done.5
  173.2 3.1 %collective-permute-start.10 = (bf16[224,384]{0,1:T(8,128)(2,1)}, bf16[224,384]{0,1:T(8,128)(2,1)S(1)}, u32[]{:S(2)}, u32[]{:S(2)}) collective-permute-start(bf16[224,384]{0,1:T(8,128)(2,1)} %copy.128), channel_id=1, source_target_pairs={{24,0},{32,8},{40,16},{48,24},{56,32},{64,40},{72,48},{80,56},{88,... | collective-permute-start | bytes 516104 | tf_op jit(solution)/shard_map/ppermute | solution.py:19
  176.3 0.7 fusion.59
  177.0 0.1 fusion.75
  177.1 1.9 collective-permute-start.11
  179.1 1.9 collective-permute-start.12
  181.0 1.9 collective-permute-start.13
  183.0 2.9 %collective-permute-start.14 = (bf16[224,384]{0,1:T(8,128)(2,1)}, bf16[224,384]{0,1:T(8,128)(2,1)}, u32[]{:S(2)}, u32[]{:S(2)}) collective-permute-start(bf16[224,384]{0,1:T(8,128)(2,1)} %copy.128), channel_id=1, source_target_pairs={{8,0},{16,8},{24,16},{32,24},{40,32},{48,40},{56,48},{64,56},{72,6... | collective-permute-start | bytes 516104 | tf_op jit(solution)/shard_map/ppermute | solution.py:19
  185.9 3.1 %collective-permute-done.10 = bf16[224,384]{0,1:T(8,128)(2,1)S(1)} collective-permute-done((bf16[224,384]{0,1:T(8,128)(2,1)}, bf16[224,384]{0,1:T(8,128)(2,1)S(1)}, u32[]{:S(2)}, u32[]{:S(2)}) %collective-permute-start.10) | collective-permute-done | bytes 172064 | tf_op jit(solution)/shard_map/ppermute | solution.py:19
  189.0 1.9 collective-permute-start.15
  191.0 2.8 %conditional.8 = ((f32[3,224]{1,0:T(4,128)S(1)}, f32[3,224]{1,0:T(4,128)S(1)}, f32[224,3,128]{2,0,1:T(8,128)S(1)})) conditional(s32[]{:T(128)} %convert_element_type.80, (f32[3,224]{1,0:T(4,128)S(1)}, f32[3,224]{1,0:T(4,128)S(1)}, f32[224,3,128]{2,0,1:T(8,128)S(1)}) %tuple.55, (pred[224]{0:T(512)(128)(4,1)S(1)}, bf16[224,384]{0,1:T(8,128)(2,1)}, ...), branch_computations={%region_15.16_spmd, %region_16.19_spmd} | conditional | flops 78298080 | bytes 3053824 | solution.py:48
  191.0 1.2 fusion.97
  192.3 0.1 fusion.3
  192.4 1.4 fusion.1
  193.8 2.8 %conditional.10 = ((f32[3,224]{1,0:T(4,128)S(1)}, f32[3,224]{1,0:T(4,128)S(1)}, f32[224,3,128]{2,0,1:T(8,128)S(1)})) conditional(s32[]{:T(128)} %convert_element_type.78, (f32[3,224]{1,0:T(4,128)S(1)}, f32[3,224]{1,0:T(4,128)S(1)}, f32[224,3,128]{2,0,1:T(8,128)S(1)}) %get-tuple-element.510, (pred[224]{0:T(512)(128)(4,1)S(1)}, ...), branch_computations={%region_25.26_spmd, %region_26.29_spmd} | conditional | flops 78298080 | bytes 3053824 | solution.py:48
  193.8 1.2 fusion.99
  195.1 0.1 fusion.17
  195.2 1.4 fusion.15
  196.6 2.8 %conditional.12 = ((f32[3,224]{1,0:T(4,128)S(1)}, f32[3,224]{1,0:T(4,128)S(1)}, f32[224,3,128]{2,0,1:T(8,128)S(1)})) conditional(s32[]{:T(128)} %convert_element_type.76, (f32[3,224]{1,0:T(4,128)S(1)}, f32[3,224]{1,0:T(4,128)S(1)}, f32[224,3,128]{2,0,1:T(8,128)S(1)}) %get-tuple-element.512, (pred[224]{0:T(512)(128)(4,1)S(1)}, ...), branch_computations={%region_35.36_spmd, %region_36.39_spmd} | conditional | flops 78298080 | bytes 3053824 | solution.py:48
  196.7 1.2 fusion.101
  197.9 0.1 fusion.31
  198.1 1.4 fusion.29
  199.4 2.8 %conditional.13 = ((f32[3,224]{1,0:T(4,128)S(1)}, f32[3,224]{1,0:T(4,128)S(1)}, f32[224,3,128]{2,0,1:T(8,128)S(1)})) conditional(s32[]{:T(128)} %convert_element_type.75, (f32[3,224]{1,0:T(4,128)S(1)}, f32[3,224]{1,0:T(4,128)S(1)}, f32[224,3,128]{2,0,1:T(8,128)S(1)}) %get-tuple-element.513, (pred[224]{0:T(512)(128)(4,1)S(1)}, ...), branch_computations={%region_40.41_spmd, %region_41.44_spmd} | conditional | flops 78298080 | bytes 3053824 | solution.py:48
  199.5 1.2 fusion.102
  200.7 0.1 fusion.38
  200.9 1.4 fusion.36
  202.3 2.8 %conditional.14 = ((f32[3,224]{1,0:T(4,128)S(1)}, f32[3,224]{1,0:T(4,128)S(1)}, f32[224,3,128]{2,0,1:T(8,128)S(1)})) conditional(s32[]{:T(128)} %convert_element_type.74, (f32[3,224]{1,0:T(4,128)S(1)}, f32[3,224]{1,0:T(4,128)S(1)}, f32[224,3,128]{2,0,1:T(8,128)S(1)}) %get-tuple-element.514, (pred[224,8]{0,1:T(8,128)(4,1)S(1)}, ...), branch_computations={%region_44.45_spmd, %region_45.49_spmd} | conditional | flops 78299648 | bytes 3055841 | solution.py:48
  202.3 1.2 fusion.103
  203.6 0.1 fusion.45
  203.7 1.4 fusion.43
  205.1 1.9 conditional.15
  205.2 1.2 fusion.104
  206.6 0.4 fusion.50
  207.0 0.2 divide_convert_fusion
  207.2 0.1 copy.160
  207.3 2.0 fusion.56
  209.3 2.6 copy.198
  212.0 49.1 %reduce-scatter.4.cloned.1.call-done = bf16[384,224]{1,0:T(8,128)(2,1)} async-done(((bf16[3072,224]{1,0:T(8,128)(2,1)}), bf16[384,224]{1,0:T(8,128)(2,1)}) %reduce-scatter.4.cloned.1.call-update) | async-done | bytes 172048
  261.1 1.1 copy.199
  262.2 0.7 fusion.77
  (76 shorter events, 0.6 us)
Async XLA Ops:
  6.5 200.8 %copy-start = (bf16[384,3072]{1,0:T(8,128)(2,1)S(1)}, bf16[384,3072]{1,0:T(8,128)(2,1)}, u32[]{:S(2)}) copy-start(bf16[384,3072]{1,0:T(8,128)(2,1)} %param.35) | copy-start | bytes 7077892
  6.5 20.5 %copy-start.2 = (bf16[1,1024,384]{2,1,0:T(8,128)(2,1)S(1)}, bf16[1,1024,384]{2,1,0:T(8,128)(2,1)}, u32[]{:S(2)}) copy-start(bf16[1,1024,384]{2,1,0:T(8,128)(2,1)} %param.31) | copy-start | bytes 2359300
  6.5 145.0 %all-reduce.3.cloned.1.call-start = ((), (), s32[]{:S(2)}) async-start(), calls=%async_computation.2 | async-start | bytes 3145728 | tf_op jit(solution)/shard_map/psum | solution.py:13
  8.4 146.1 %collective-permute-start = (bf16[224,384]{0,1:T(8,128)(2,1)}, bf16[224,384]{0,1:T(8,128)(2,1)}, u32[]{:S(2)}, u32[]{:S(2)}) collective-permute-start(bf16[224,384]{0,1:T(8,128)(2,1)} %copy.128), channel_id=1, source_target_pairs={{0,8},{8,16},{16,24},{24,32},{32,40},{40,48},{48,56},{56,64},{64,7... | collective-permute-start | bytes 516104 | tf_op jit(solution)/shard_map/ppermute | solution.py:19
  10.3 151.9 %collective-permute-start.2 = (bf16[224,384]{0,1:T(8,128)(2,1)}, bf16[224,384]{0,1:T(8,128)(2,1)}, u32[]{:S(2)}, u32[]{:S(2)}) collective-permute-start(bf16[224,384]{0,1:T(8,128)(2,1)} %copy.128), channel_id=1, source_target_pairs={{0,16},{8,24},{16,32},{24,40},{32,48},{40,56},{48,64},{56,72},{64,... | collective-permute-start | bytes 516104 | tf_op jit(solution)/shard_map/ppermute | solution.py:19
  14.9 141.9 %collective-permute-start.1 = (bf16[224,384]{0,1:T(8,128)(2,1)S(1)}, bf16[224,384]{0,1:T(8,128)(2,1)}, u32[]{:S(2)}, u32[]{:S(2)}) collective-permute-start(bf16[224,384]{0,1:T(8,128)(2,1)S(1)} %copy.133), channel_id=1, source_target_pairs={{0,8},{8,16},{16,24},{24,32},{32,40},{40,48},{48,56},{56,64},{64,7... | collective-permute-start | bytes 516104 | tf_op jit(solution)/shard_map/ppermute | solution.py:19
  18.2 146.9 %collective-permute-start.3 = (bf16[224,384]{0,1:T(8,128)(2,1)S(1)}, bf16[224,384]{0,1:T(8,128)(2,1)}, u32[]{:S(2)}, u32[]{:S(2)}) collective-permute-start(bf16[224,384]{0,1:T(8,128)(2,1)S(1)} %copy.133), channel_id=1, source_target_pairs={{0,16},{8,24},{16,32},{24,40},{32,48},{40,56},{48,64},{56,72},{64,... | collective-permute-start | bytes 516104 | tf_op jit(solution)/shard_map/ppermute | solution.py:19
  21.4 149.2 %collective-permute-start.4 = (bf16[224,384]{0,1:T(8,128)(2,1)}, bf16[224,384]{0,1:T(8,128)(2,1)}, u32[]{:S(2)}, u32[]{:S(2)}) collective-permute-start(bf16[224,384]{0,1:T(8,128)(2,1)} %copy.128), channel_id=1, source_target_pairs={{0,24},{8,32},{16,40},{24,48},{32,56},{40,64},{48,72},{56,80},{64,... | collective-permute-start | bytes 516104 | tf_op jit(solution)/shard_map/ppermute | solution.py:19
  32.7 228.4 %reduce-scatter.4.cloned.1.call-start = ((), (), s32[]{:S(2)}) async-start(), calls=%async_computation.1 | async-start | bytes 1769472
  151.6 1.9 copy-start.13
  153.4 3.0 %copy-start.1 = (f32[3,224,224]{1,2,0:T(8,128)S(1)}, f32[3,224,224]{1,2,0:T(8,128)}, u32[]{:S(2)}) copy-start(f32[3,224,224]{1,2,0:T(8,128)} %get-tuple-element.450) | copy-start | bytes 1806340
  154.5 36.5 %copy-start.12 = (pred[224]{0:T(512)(128)(4,1)S(1)}, pred[224]{0:T(512)(128)(4,1)}, u32[]{:S(2)}) copy-start(pred[224]{0:T(512)(128)(4,1)} %get-tuple-element.394) | copy-start | bytes 676
  154.5 18.1 %collective-permute-start.5 = (bf16[224,384]{0,1:T(8,128)(2,1)S(1)}, bf16[224,384]{0,1:T(8,128)(2,1)S(1)}, u32[]{:S(2)}, u32[]{:S(2)}) collective-permute-start(bf16[224,384]{0,1:T(8,128)(2,1)S(1)} %copy.133), channel_id=1, source_target_pairs={{0,24},{8,32},{16,40},{24,48},{32,56},{40,64},{48,72},{56,80},{64,... | collective-permute-start | bytes 516104 | tf_op jit(solution)/shard_map/ppermute | solution.py:19
  156.8 20.3 %collective-permute-start.6 = (bf16[224,384]{0,1:T(8,128)(2,1)}, bf16[224,384]{0,1:T(8,128)(2,1)S(1)}, u32[]{:S(2)}, u32[]{:S(2)}) collective-permute-start(bf16[224,384]{0,1:T(8,128)(2,1)} %copy.128), channel_id=1, source_target_pairs={{0,32},{8,40},{16,48},{24,56},{32,64},{40,72},{48,80},{56,88},{64,... | collective-permute-start | bytes 516104 | tf_op jit(solution)/shard_map/ppermute | solution.py:19
  162.3 16.8 %collective-permute-start.7 = (bf16[224,384]{0,1:T(8,128)(2,1)S(1)}, bf16[224,384]{0,1:T(8,128)(2,1)S(1)}, u32[]{:S(2)}, u32[]{:S(2)}) collective-permute-start(bf16[224,384]{0,1:T(8,128)(2,1)S(1)} %copy.133), channel_id=1, source_target_pairs={{0,32},{8,40},{16,48},{24,56},{32,64},{40,72},{48,80},{56,88},{64,... | collective-permute-start | bytes 516104 | tf_op jit(solution)/shard_map/ppermute | solution.py:19
  165.1 15.9 %collective-permute-start.8 = (bf16[224,384]{0,1:T(8,128)(2,1)}, bf16[224,384]{0,1:T(8,128)(2,1)S(1)}, u32[]{:S(2)}, u32[]{:S(2)}) collective-permute-start(bf16[224,384]{0,1:T(8,128)(2,1)} %copy.128), channel_id=1, source_target_pairs={{32,0},{40,8},{48,16},{56,24},{64,32},{72,40},{80,48},{88,56},{96,... | collective-permute-start | bytes 516104 | tf_op jit(solution)/shard_map/ppermute | solution.py:19
  170.6 12.3 %collective-permute-start.9 = (bf16[224,384]{0,1:T(8,128)(2,1)S(1)}, bf16[224,384]{0,1:T(8,128)(2,1)S(1)}, u32[]{:S(2)}, u32[]{:S(2)}) collective-permute-start(bf16[224,384]{0,1:T(8,128)(2,1)S(1)} %copy.133), channel_id=1, source_target_pairs={{32,0},{40,8},{48,16},{56,24},{64,32},{72,40},{80,48},{88,56},{96,... | collective-permute-start | bytes 516104 | tf_op jit(solution)/shard_map/ppermute | solution.py:19
  172.5 0.7 copy-start.5
  173.2 15.8 %collective-permute-start.10 = (bf16[224,384]{0,1:T(8,128)(2,1)}, bf16[224,384]{0,1:T(8,128)(2,1)S(1)}, u32[]{:S(2)}, u32[]{:S(2)}) collective-permute-start(bf16[224,384]{0,1:T(8,128)(2,1)} %copy.128), channel_id=1, source_target_pairs={{24,0},{32,8},{40,16},{48,24},{56,32},{64,40},{72,48},{80,56},{88,... | collective-permute-start | bytes 516104 | tf_op jit(solution)/shard_map/ppermute | solution.py:19
  177.0 16.8 %copy-start.11 = (pred[224]{0:T(512)(128)(4,1)S(1)}, pred[224]{0:T(512)(128)(4,1)}, u32[]{:S(2)}) copy-start(pred[224]{0:T(512)(128)(4,1)} %get-tuple-element.396) | copy-start | bytes 676
  177.1 13.9 %copy-start.8 = (bf16[224,384]{0,1:T(8,128)(2,1)}, bf16[224,384]{0,1:T(8,128)(2,1)S(1)}, u32[]{:S(2)}) copy-start(bf16[224,384]{0,1:T(8,128)(2,1)S(1)} %collective-permute-done.6) | copy-start | bytes 516100
  177.1 22.3 %collective-permute-start.11 = (bf16[224,384]{0,1:T(8,128)(2,1)S(1)}, bf16[224,384]{0,1:T(8,128)(2,1)}, u32[]{:S(2)}, u32[]{:S(2)}) collective-permute-start(bf16[224,384]{0,1:T(8,128)(2,1)S(1)} %copy.133), channel_id=1, source_target_pairs={{24,0},{32,8},{40,16},{48,24},{56,32},{64,40},{72,48},{80,56},{88,... | collective-permute-start | bytes 516104 | tf_op jit(solution)/shard_map/ppermute | solution.py:19
  179.1 6.8 %copy-start.4 = (bf16[224,384]{0,1:T(8,128)(2,1)}, bf16[224,384]{0,1:T(8,128)(2,1)S(1)}, u32[]{:S(2)}) copy-start(bf16[224,384]{0,1:T(8,128)(2,1)S(1)} %collective-permute-done.7) | copy-start | bytes 516100
  179.1 23.2 %collective-permute-start.12 = (bf16[224,384]{0,1:T(8,128)(2,1)}, bf16[224,384]{0,1:T(8,128)(2,1)}, u32[]{:S(2)}, u32[]{:S(2)}) collective-permute-start(bf16[224,384]{0,1:T(8,128)(2,1)} %copy.128), channel_id=1, source_target_pairs={{16,0},{24,8},{32,16},{40,24},{48,32},{56,40},{64,48},{72,56},{80,... | collective-permute-start | bytes 516104 | tf_op jit(solution)/shard_map/ppermute | solution.py:19
  181.0 10.0 %copy-start.7 = (bf16[224,384]{0,1:T(8,128)(2,1)}, bf16[224,384]{0,1:T(8,128)(2,1)S(1)}, u32[]{:S(2)}) copy-start(bf16[224,384]{0,1:T(8,128)(2,1)S(1)} %collective-permute-done.8) | copy-start | bytes 516100
  181.0 21.2 %collective-permute-start.13 = (bf16[224,384]{0,1:T(8,128)(2,1)S(1)}, bf16[224,384]{0,1:T(8,128)(2,1)}, u32[]{:S(2)}, u32[]{:S(2)}) collective-permute-start(bf16[224,384]{0,1:T(8,128)(2,1)S(1)} %copy.133), channel_id=1, source_target_pairs={{16,0},{24,8},{32,16},{40,24},{48,32},{56,40},{64,48},{72,56},{80,... | collective-permute-start | bytes 516104 | tf_op jit(solution)/shard_map/ppermute | solution.py:19
  183.0 2.9 %copy-start.3 = (bf16[224,384]{0,1:T(8,128)(2,1)}, bf16[224,384]{0,1:T(8,128)(2,1)S(1)}, u32[]{:S(2)}) copy-start(bf16[224,384]{0,1:T(8,128)(2,1)S(1)} %collective-permute-done.9) | copy-start | bytes 516100
  183.0 22.1 %collective-permute-start.14 = (bf16[224,384]{0,1:T(8,128)(2,1)}, bf16[224,384]{0,1:T(8,128)(2,1)}, u32[]{:S(2)}, u32[]{:S(2)}) collective-permute-start(bf16[224,384]{0,1:T(8,128)(2,1)} %copy.128), channel_id=1, source_target_pairs={{8,0},{16,8},{24,16},{32,24},{40,32},{48,40},{56,48},{64,56},{72,6... | collective-permute-start | bytes 516104 | tf_op jit(solution)/shard_map/ppermute | solution.py:19
  189.0 1.9 copy-start.6
  189.0 16.1 %collective-permute-start.15 = (bf16[224,384]{0,1:T(8,128)(2,1)S(1)}, bf16[224,384]{0,1:T(8,128)(2,1)S(1)}, u32[]{:S(2)}, u32[]{:S(2)}) collective-permute-start(bf16[224,384]{0,1:T(8,128)(2,1)S(1)} %copy.133), channel_id=1, source_target_pairs={{8,0},{16,8},{24,16},{32,24},{40,32},{48,40},{56,48},{64,56},{72,6... | collective-permute-start | bytes 516104 | tf_op jit(solution)/shard_map/ppermute | solution.py:19
  209.3 52.8 %copy-start.9 = (bf16[224,384]{1,0:T(8,128)(2,1)S(1)}, bf16[224,384]{1,0:T(8,128)(2,1)}, u32[]{:S(2)}) copy-start(bf16[224,384]{1,0:T(8,128)(2,1)} %param.36) | copy-start | bytes 516100
  209.3 52.8 %copy-start.10 = (f32[384]{0:T(512)S(1)}, f32[384]{0:T(512)}, u32[]{:S(2)}) copy-start(f32[384]{0:T(512)} %param.37) | copy-start | bytes 4612
Sparse Core Ops, SparseCore 0:
  32.8 118.6 all-reduce.2
  212.1 48.9 reduce-scatter.3
where the time goes:
time: 271 us; the launch traced here: 270 us
  waiting for transfers between devices  161 us (59%)
  starting transfers between devices  45.9 us (17%)
  matrix products  21.9 us (8%)
  between operations  20.2 us (7%)
  local copies, waits for them, and re-layouts  15.5 us (6%)
  other arithmetic  5.24 us (2%)
    psum x1, waiting for transfers between devices, broadcast(): return lax.psum(block, axis)  109 us
    unnamed x3, waiting for transfers between devices  49.2 us
    ppermute x16, starting transfers between devices, from_behind(): return lax.ppermute(block, axis, route)  45.8 us
    unnamed x35, local copies, waits for them, and re-layouts  11.9 us
    dot_general x8, matrix products, absorb(): jnp.einsum('qhd,khd->hqk', query_heads, key_heads, preferred_element_type...  11.4 us
    dot_general x8, matrix products, absorb(): jnp.einsum('hqk,khd->qhd', weights.astype(jnp.bfloat16), value_heads, pre...  8.54 us
  transfers between devices with their start and end apart: 18, of which 3 were waited for; matrix products, arithmetic and copies ran while one was open for 12% of the time, Pallas kernels for 0%

commit v1 on v0

--- a/solution.py
+++ b/solution.py
@@ -10,7 +10,7 @@
 
 def broadcast(block, axis, source):
     block = jnp.where(lax.axis_index(axis) == source, block, jnp.zeros_like(block))
-    return lax.psum(block, axis)
+    return lax.all_gather(block, axis_name=axis).sum(axis=0)
 
 
 def from_behind(block, axis, distance):

time: 271 us -> 354 us (1.31)
  waiting for transfers between devices: 161 us -> 210 us
  other arithmetic: 5.24 us -> 33.2 us
  starting transfers between devices: 45.9 us -> 54.8 us
  local copies, waits for them, and re-layouts: 15.5 us -> 9.94 us
    all_gather x0 -> x2, waiting for transfers between devices: none -> 161 us  [broadcast(): return lax.all_gather(block, axis_name=axis).sum(axis=0)]
    psum x1 -> x0, waiting for transfers between devices: 109 us -> none  [broadcast(): return lax.psum(block, axis)]
    reduce_sum x0 -> x2, other arithmetic: none -> 27.6 us  [broadcast(): return lax.all_gather(block, axis_name=axis).sum(axis=0)]
    ppermute x16, starting transfers between devices: 45.8 us -> 54.7 us  [from_behind(): return lax.ppermute(block, axis, route)]
    unnamed x35 -> x37, local copies, waits for them, and re-layouts: 11.9 us -> 5.13 us
    reduce_sum x0 -> x2, local copies, waits for them, and re-layouts: none -> 4.65 us  [broadcast(): return lax.all_gather(block, axis_name=axis).sum(axis=0)]
    unnamed x3 -> x4, waiting for transfers between devices: 49.2 us -> 49 us
  transfers between devices with their start and end apart: 18 -> 19, of which waited for: 3 -> 3; matrix products, arithmetic and copies ran while one was open for 12% -> 16% of each run, Pallas kernels for 0% -> 0%
where the time goes in v1:
time: 354 us; the launch traced here: 353 us
  waiting for transfers between devices  210 us (59%)
  starting transfers between devices  54.8 us (15%)
  other arithmetic  33.2 us (9%)
  matrix products  24.5 us (7%)
  between operations  20.3 us (6%)
  local copies, waits for them, and re-layouts  9.94 us (3%)
    all_gather x2, waiting for transfers between devices, broadcast(): return lax.all_gather(block, axis_name=axis).sum(axis=0)  161 us
    ppermute x16, starting transfers between devices, from_behind(): return lax.ppermute(block, axis, route)  54.7 us
    unnamed x4, waiting for transfers between devices  49 us
    reduce_sum x2, other arithmetic, broadcast(): return lax.all_gather(block, axis_name=axis).sum(axis=0)  27.6 us
    dot_general x8, matrix products, absorb(): jnp.einsum('qhd,khd->hqk', query_heads, key_heads, preferred_element_type...  12 us
    dot_general x8, matrix products, absorb(): jnp.einsum('hqk,khd->qhd', weights.astype(jnp.bfloat16), value_heads, pre...  10.5 us
  transfers between devices with their start and end apart: 19, of which 3 were waited for; matrix products, arithmetic and copies ran while one was open for 16% of the time, Pallas kernels for 0%

profile of v1, /device:TPU:2, one launch (start us, length us, event | category | flops | bytes accessed | tf_op | source)
XLA Modules:
  0.0 353.1 jit_solution(2810025348053548197)
XLA Ops:
  7.4 1.0 broadcast_select_fusion.1
  8.4 1.0 broadcast_select_fusion
  9.5 0.1 copy.126
  9.7 1.9 collective-permute-start
  11.6 3.5 collective-permute-start.2
  15.1 0.1 copy.131
  15.2 3.3 collective-permute-start.1
  18.5 3.2 collective-permute-start.3
  21.7 5.0 %collective-permute-start.4 = (bf16[224,384]{0,1:T(8,128)(2,1)S(1)}, bf16[224,384]{0,1:T(8,128)(2,1)}, u32[]{:S(2)}, u32[]{:S(2)}) collective-permute-start(bf16[224,384]{0,1:T(8,128)(2,1)S(1)} %copy.126), channel_id=1, source_target_pairs={{0,24},{8,32},{16,40},{24,48},{32,56},{40,64},{48,72},{56,80},{64,... | collective-permute-start | bytes 516104 | tf_op jit(solution)/shard_map/ppermute | solution.py:19
  26.8 1.1 copy.123
  28.6 0.9 fusion.89
  34.6 1.2 fusion.105
  35.8 81.3 %all-gather.5.cloned.1.call-done = bf16[32,1024,384]{2,1,0:T(8,128)(2,1)} async-done(((bf16[1,1024,384]{2,1,0:T(8,128)(2,1)}), bf16[32,1024,384]{2,1,0:T(8,128)(2,1)}) %all-gather.5.cloned.1.call-update) | async-done | bytes 25165840 | tf_op jit(solution)/shard_map/all_gather | solution.py:13
  117.1 13.8 %reduce.12 = bf16[1024,384]{1,0:T(8,128)(2,1)} reduce(bf16[32,1024,384]{2,1,0:T(8,128)(2,1)} %all-gather.5.cloned.1.call-done, bf16[]{:T(256)} %constant.122.clone.1), dimensions={0}, to_apply=%region_8.9 | reduce | flops 12189696 | bytes 25952258 | tf_op jit(solution)/shard_map/reduce_sum | solution.py:13
  130.9 2.4 copy.122
  133.3 3.4 bitcast_reduce_fusion
  136.7 79.6 %all-gather.7.cloned.1.call-done = bf16[32,1024,384]{2,1,0:T(8,128)(2,1)} async-done(((bf16[1,1024,384]{2,1,0:T(8,128)(2,1)}), bf16[32,1024,384]{2,1,0:T(8,128)(2,1)}) %all-gather.7.cloned.1.call-update) | async-done | bytes 25165840 | tf_op jit(solution)/shard_map/all_gather | solution.py:13
  216.3 13.8 %reduce.13 = bf16[1024,384]{1,0:T(8,128)(2,1)} reduce(bf16[32,1024,384]{2,1,0:T(8,128)(2,1)} %all-gather.7.cloned.1.call-done, bf16[]{:T(256)} %constant.122.clone.1), dimensions={0}, to_apply=%region_13.14 | reduce | flops 12189696 | bytes 25952258 | tf_op jit(solution)/shard_map/reduce_sum | solution.py:13
  230.1 2.3 copy.129
  232.4 2.9 fusion.71
  235.3 1.9 collective-permute-start.5
  237.2 0.3 fusion.64
  237.6 4.1 %collective-permute-start.6 = (bf16[224,384]{0,1:T(8,128)(2,1)S(1)}, bf16[224,384]{0,1:T(8,128)(2,1)S(1)}, u32[]{:S(2)}, u32[]{:S(2)}) collective-permute-start(bf16[224,384]{0,1:T(8,128)(2,1)S(1)} %copy.126), channel_id=1, source_target_pairs={{0,32},{8,40},{16,48},{24,56},{32,64},{40,72},{48,80},{56,88},{64,... | collective-permute-start | bytes 516104 | tf_op jit(solution)/shard_map/ppermute | solution.py:19
  241.7 4.2 %collective-permute-start.7 = (bf16[224,384]{0,1:T(8,128)(2,1)S(1)}, bf16[224,384]{0,1:T(8,128)(2,1)S(1)}, u32[]{:S(2)}, u32[]{:S(2)}) collective-permute-start(bf16[224,384]{0,1:T(8,128)(2,1)S(1)} %copy.131), channel_id=1, source_target_pairs={{0,32},{8,40},{16,48},{24,56},{32,64},{40,72},{48,80},{56,88},{64,... | collective-permute-start | bytes 516104 | tf_op jit(solution)/shard_map/ppermute | solution.py:19
  245.9 4.0 %collective-permute-start.8 = (bf16[224,384]{0,1:T(8,128)(2,1)S(1)}, bf16[224,384]{0,1:T(8,128)(2,1)S(1)}, u32[]{:S(2)}, u32[]{:S(2)}) collective-permute-start(bf16[224,384]{0,1:T(8,128)(2,1)S(1)} %copy.126), channel_id=1, source_target_pairs={{32,0},{40,8},{48,16},{56,24},{64,32},{72,40},{80,48},{88,56},{96,... | collective-permute-start | bytes 516104 | tf_op jit(solution)/shard_map/ppermute | solution.py:19
  250.0 3.3 collective-permute-start.9
  253.3 2.0 collective-permute-start.10
  255.3 0.7 fusion.59
  256.1 1.9 collective-permute-start.11
  258.1 2.3 collective-permute-start.12
  260.4 10.1 %collective-permute-start.13 = (bf16[224,384]{0,1:T(8,128)(2,1)S(1)}, bf16[224,384]{0,1:T(8,128)(2,1)}, u32[]{:S(2)}, u32[]{:S(2)}) collective-permute-start(bf16[224,384]{0,1:T(8,128)(2,1)S(1)} %copy.131), channel_id=1, source_target_pairs={{16,0},{24,8},{32,16},{40,24},{48,32},{56,40},{64,48},{72,56},{80,... | collective-permute-start | bytes 516104 | tf_op jit(solution)/shard_map/ppermute | solution.py:19
  270.5 1.9 collective-permute-start.14
  272.5 2.0 collective-permute-start.15
  274.6 2.8 conditional.8
  274.6 1.2 fusion.97
  275.9 0.1 fusion.3
  276.0 1.4 fusion.1
  277.4 2.8 conditional.10
  277.5 1.2 fusion.99
  278.7 0.1 fusion.17
  278.9 1.4 fusion.15
  280.3 2.8 conditional.12
  280.3 1.2 fusion.101
  281.5 0.1 fusion.31
  281.7 1.4 fusion.29
  283.1 2.8 conditional.13
  283.1 1.2 fusion.102
  284.4 0.1 fusion.38
  284.5 1.4 fusion.36
  285.9 3.0 conditional.14
  286.1 1.2 fusion.103
  287.4 0.1 fusion.45
  287.5 1.4 fusion.43
  288.9 1.9 conditional.15
  289.0 1.2 fusion.104
  290.2 0.1 fusion.52
  290.4 0.4 fusion.50
  290.8 0.2 divide_convert_fusion
  291.0 0.1 copy.158
  291.1 2.0 fusion.56
  293.1 2.6 copy.198
  295.8 49.0 %reduce-scatter.4.cloned.1.call-done = bf16[384,224]{1,0:T(8,128)(2,1)} async-done(((bf16[3072,224]{1,0:T(8,128)(2,1)}), bf16[384,224]{1,0:T(8,128)(2,1)}) %reduce-scatter.4.cloned.1.call-update) | async-done | bytes 172048
  344.8 1.1 copy.199
  345.9 0.7 fusion.77
  (84 shorter events, 0.7 us)
Async XLA Ops:
  6.5 284.6 %copy-start = (bf16[384,3072]{1,0:T(8,128)(2,1)S(1)}, bf16[384,3072]{1,0:T(8,128)(2,1)}, u32[]{:S(2)}) copy-start(bf16[384,3072]{1,0:T(8,128)(2,1)} %param.35) | copy-start | bytes 7077892
  6.5 3.0 copy-start.11
  6.5 8.5 %copy-start.12 = (bf16[224,384]{1,0:T(8,128)(2,1)S(1)}, bf16[224,384]{1,0:T(8,128)(2,1)}, u32[]{:S(2)}) copy-start(bf16[224,384]{1,0:T(8,128)(2,1)} %param.29) | copy-start | bytes 516100
  6.5 110.6 %all-gather.5.cloned.1.call-start = ((), (), s32[]{:S(2)}) async-start(), calls=%async_computation.1 | async-start | bytes 25952256 | tf_op jit(solution)/shard_map/all_gather | solution.py:13
  7.3 21.3 %copy-start.15 = (s32[1,8]{1,0:T(1,128)S(1)}, s32[1,8]{1,0:T(1,128)}, u32[]{:S(2)}) copy-start(s32[1,8]{1,0:T(1,128)} %param.32) | copy-start | bytes 100
  8.4 207.9 %all-gather.7.cloned.1.call-start = ((), (), s32[]{:S(2)}) async-start(), calls=%async_computation.2 | async-start | bytes 25952256 | tf_op jit(solution)/shard_map/all_gather | solution.py:13
  9.4 335.3 %reduce-scatter.4.cloned.1.call-start = ((), (), s32[]{:S(2)}) async-start(), calls=%async_computation.3 | async-start | bytes 1769472
  9.7 225.6 %collective-permute-start = (bf16[224,384]{0,1:T(8,128)(2,1)S(1)}, bf16[224,384]{0,1:T(8,128)(2,1)S(1)}, u32[]{:S(2)}, u32[]{:S(2)}) collective-permute-start(bf16[224,384]{0,1:T(8,128)(2,1)S(1)} %copy.126), channel_id=1, source_target_pairs={{0,8},{8,16},{16,24},{24,32},{32,40},{40,48},{48,56},{56,64},{64,7... | collective-permute-start | bytes 516104 | tf_op jit(solution)/shard_map/ppermute | solution.py:19
  11.6 230.1 %collective-permute-start.2 = (bf16[224,384]{0,1:T(8,128)(2,1)S(1)}, bf16[224,384]{0,1:T(8,128)(2,1)}, u32[]{:S(2)}, u32[]{:S(2)}) collective-permute-start(bf16[224,384]{0,1:T(8,128)(2,1)S(1)} %copy.126), channel_id=1, source_target_pairs={{0,16},{8,24},{16,32},{24,40},{32,48},{40,56},{48,64},{56,72},{64,... | collective-permute-start | bytes 516104 | tf_op jit(solution)/shard_map/ppermute | solution.py:19
  15.2 222.4 %collective-permute-start.1 = (bf16[224,384]{0,1:T(8,128)(2,1)S(1)}, bf16[224,384]{0,1:T(8,128)(2,1)}, u32[]{:S(2)}, u32[]{:S(2)}) collective-permute-start(bf16[224,384]{0,1:T(8,128)(2,1)S(1)} %copy.131), channel_id=1, source_target_pairs={{0,8},{8,16},{16,24},{24,32},{32,40},{40,48},{48,56},{56,64},{64,7... | collective-permute-start | bytes 516104 | tf_op jit(solution)/shard_map/ppermute | solution.py:19
  18.5 227.3 %collective-permute-start.3 = (bf16[224,384]{0,1:T(8,128)(2,1)S(1)}, bf16[224,384]{0,1:T(8,128)(2,1)S(1)}, u32[]{:S(2)}, u32[]{:S(2)}) collective-permute-start(bf16[224,384]{0,1:T(8,128)(2,1)S(1)} %copy.131), channel_id=1, source_target_pairs={{0,16},{8,24},{16,32},{24,40},{32,48},{40,56},{48,64},{56,72},{64,... | collective-permute-start | bytes 516104 | tf_op jit(solution)/shard_map/ppermute | solution.py:19
  21.7 228.2 %collective-permute-start.4 = (bf16[224,384]{0,1:T(8,128)(2,1)S(1)}, bf16[224,384]{0,1:T(8,128)(2,1)}, u32[]{:S(2)}, u32[]{:S(2)}) collective-permute-start(bf16[224,384]{0,1:T(8,128)(2,1)S(1)} %copy.126), channel_id=1, source_target_pairs={{0,24},{8,32},{16,40},{24,48},{32,56},{40,64},{48,72},{56,80},{64,... | collective-permute-start | bytes 516104 | tf_op jit(solution)/shard_map/ppermute | solution.py:19
  232.4 4.9 %copy-start.2 = (f32[3,224,224]{1,2,0:T(8,128)S(1)}, f32[3,224,224]{1,2,0:T(8,128)}, u32[]{:S(2)}) copy-start(f32[3,224,224]{1,2,0:T(8,128)} %get-tuple-element.448) | copy-start | bytes 1806340
  232.4 22.9 %copy-start.1 = (f32[3,1024,224]{1,2,0:T(8,128)S(1)}, f32[3,1024,224]{1,2,0:T(8,128)}, u32[]{:S(2)}) copy-start(f32[3,1024,224]{1,2,0:T(8,128)} %get-tuple-element.446) | copy-start | bytes 8257540
  235.3 1.9 copy-start.8
  235.3 18.0 %collective-permute-start.5 = (bf16[224,384]{0,1:T(8,128)(2,1)S(1)}, bf16[224,384]{0,1:T(8,128)(2,1)S(1)}, u32[]{:S(2)}, u32[]{:S(2)}) collective-permute-start(bf16[224,384]{0,1:T(8,128)(2,1)S(1)} %copy.131), channel_id=1, source_target_pairs={{0,24},{8,32},{16,40},{24,48},{32,56},{40,64},{48,72},{56,80},{64,... | collective-permute-start | bytes 516104 | tf_op jit(solution)/shard_map/ppermute | solution.py:19
  237.6 18.5 %collective-permute-start.6 = (bf16[224,384]{0,1:T(8,128)(2,1)S(1)}, bf16[224,384]{0,1:T(8,128)(2,1)S(1)}, u32[]{:S(2)}, u32[]{:S(2)}) collective-permute-start(bf16[224,384]{0,1:T(8,128)(2,1)S(1)} %copy.126), channel_id=1, source_target_pairs={{0,32},{8,40},{16,48},{24,56},{32,64},{40,72},{48,80},{56,88},{64,... | collective-permute-start | bytes 516104 | tf_op jit(solution)/shard_map/ppermute | solution.py:19
  241.7 16.4 %collective-permute-start.7 = (bf16[224,384]{0,1:T(8,128)(2,1)S(1)}, bf16[224,384]{0,1:T(8,128)(2,1)S(1)}, u32[]{:S(2)}, u32[]{:S(2)}) collective-permute-start(bf16[224,384]{0,1:T(8,128)(2,1)S(1)} %copy.131), channel_id=1, source_target_pairs={{0,32},{8,40},{16,48},{24,56},{32,64},{40,72},{48,80},{56,88},{64,... | collective-permute-start | bytes 516104 | tf_op jit(solution)/shard_map/ppermute | solution.py:19
  245.9 26.6 %copy-start.3 = (bf16[224,384]{0,1:T(8,128)(2,1)}, bf16[224,384]{0,1:T(8,128)(2,1)S(1)}, u32[]{:S(2)}) copy-start(bf16[224,384]{0,1:T(8,128)(2,1)S(1)} %collective-permute-done.3) | copy-start | bytes 516100
  245.9 14.5 %collective-permute-start.8 = (bf16[224,384]{0,1:T(8,128)(2,1)S(1)}, bf16[224,384]{0,1:T(8,128)(2,1)S(1)}, u32[]{:S(2)}, u32[]{:S(2)}) collective-permute-start(bf16[224,384]{0,1:T(8,128)(2,1)S(1)} %copy.126), channel_id=1, source_target_pairs={{32,0},{40,8},{48,16},{56,24},{64,32},{72,40},{80,48},{88,56},{96,... | collective-permute-start | bytes 516104 | tf_op jit(solution)/shard_map/ppermute | solution.py:19
  250.0 20.6 %collective-permute-start.9 = (bf16[224,384]{0,1:T(8,128)(2,1)S(1)}, bf16[224,384]{0,1:T(8,128)(2,1)S(1)}, u32[]{:S(2)}, u32[]{:S(2)}) collective-permute-start(bf16[224,384]{0,1:T(8,128)(2,1)S(1)} %copy.131), channel_id=1, source_target_pairs={{32,0},{40,8},{48,16},{56,24},{64,32},{72,40},{80,48},{88,56},{96,... | collective-permute-start | bytes 516104 | tf_op jit(solution)/shard_map/ppermute | solution.py:19
  253.3 21.3 %copy-start.6 = (bf16[224,384]{0,1:T(8,128)(2,1)}, bf16[224,384]{0,1:T(8,128)(2,1)S(1)}, u32[]{:S(2)}) copy-start(bf16[224,384]{0,1:T(8,128)(2,1)S(1)} %collective-permute-done.5) | copy-start | bytes 516100
  253.3 19.2 %collective-permute-start.10 = (bf16[224,384]{0,1:T(8,128)(2,1)S(1)}, bf16[224,384]{0,1:T(8,128)(2,1)S(1)}, u32[]{:S(2)}, u32[]{:S(2)}) collective-permute-start(bf16[224,384]{0,1:T(8,128)(2,1)S(1)} %copy.126), channel_id=1, source_target_pairs={{24,0},{32,8},{40,16},{48,24},{56,32},{64,40},{72,48},{80,56},{88,... | collective-permute-start | bytes 516104 | tf_op jit(solution)/shard_map/ppermute | solution.py:19
  256.1 18.5 %copy-start.10 = (bf16[224,384]{0,1:T(8,128)(2,1)}, bf16[224,384]{0,1:T(8,128)(2,1)S(1)}, u32[]{:S(2)}) copy-start(bf16[224,384]{0,1:T(8,128)(2,1)S(1)} %collective-permute-done.6) | copy-start | bytes 516100
  256.1 26.9 %collective-permute-start.11 = (bf16[224,384]{0,1:T(8,128)(2,1)S(1)}, bf16[224,384]{0,1:T(8,128)(2,1)}, u32[]{:S(2)}, u32[]{:S(2)}) collective-permute-start(bf16[224,384]{0,1:T(8,128)(2,1)S(1)} %copy.131), channel_id=1, source_target_pairs={{24,0},{32,8},{40,16},{48,24},{56,32},{64,40},{72,48},{80,56},{88,... | collective-permute-start | bytes 516104 | tf_op jit(solution)/shard_map/ppermute | solution.py:19
  258.1 16.5 %copy-start.5 = (bf16[224,384]{0,1:T(8,128)(2,1)}, bf16[224,384]{0,1:T(8,128)(2,1)S(1)}, u32[]{:S(2)}) copy-start(bf16[224,384]{0,1:T(8,128)(2,1)S(1)} %collective-permute-done.7) | copy-start | bytes 516100
  258.1 27.8 %collective-permute-start.12 = (bf16[224,384]{0,1:T(8,128)(2,1)S(1)}, bf16[224,384]{0,1:T(8,128)(2,1)}, u32[]{:S(2)}, u32[]{:S(2)}) collective-permute-start(bf16[224,384]{0,1:T(8,128)(2,1)S(1)} %copy.126), channel_id=1, source_target_pairs={{16,0},{24,8},{32,16},{40,24},{48,32},{56,40},{64,48},{72,56},{80,... | collective-permute-start | bytes 516104 | tf_op jit(solution)/shard_map/ppermute | solution.py:19
  260.4 14.2 %copy-start.9 = (bf16[224,384]{0,1:T(8,128)(2,1)}, bf16[224,384]{0,1:T(8,128)(2,1)S(1)}, u32[]{:S(2)}) copy-start(bf16[224,384]{0,1:T(8,128)(2,1)S(1)} %collective-permute-done.8) | copy-start | bytes 516100
  260.4 25.5 %collective-permute-start.13 = (bf16[224,384]{0,1:T(8,128)(2,1)S(1)}, bf16[224,384]{0,1:T(8,128)(2,1)}, u32[]{:S(2)}, u32[]{:S(2)}) collective-permute-start(bf16[224,384]{0,1:T(8,128)(2,1)S(1)} %copy.131), channel_id=1, source_target_pairs={{16,0},{24,8},{32,16},{40,24},{48,32},{56,40},{64,48},{72,56},{80,... | collective-permute-start | bytes 516104 | tf_op jit(solution)/shard_map/ppermute | solution.py:19
  270.5 4.0 %copy-start.4 = (bf16[224,384]{0,1:T(8,128)(2,1)}, bf16[224,384]{0,1:T(8,128)(2,1)S(1)}, u32[]{:S(2)}) copy-start(bf16[224,384]{0,1:T(8,128)(2,1)S(1)} %collective-permute-done.9) | copy-start | bytes 516100
  270.5 18.4 %collective-permute-start.14 = (bf16[224,384]{0,1:T(8,128)(2,1)S(1)}, bf16[224,384]{0,1:T(8,128)(2,1)}, u32[]{:S(2)}, u32[]{:S(2)}) collective-permute-start(bf16[224,384]{0,1:T(8,128)(2,1)S(1)} %copy.126), channel_id=1, source_target_pairs={{8,0},{16,8},{24,16},{32,24},{40,32},{48,40},{56,48},{64,56},{72,6... | collective-permute-start | bytes 516104 | tf_op jit(solution)/shard_map/ppermute | solution.py:19
  272.5 2.1 copy-start.7
  272.5 16.4 %collective-permute-start.15 = (bf16[224,384]{0,1:T(8,128)(2,1)S(1)}, bf16[224,384]{0,1:T(8,128)(2,1)S(1)}, u32[]{:S(2)}, u32[]{:S(2)}) collective-permute-start(bf16[224,384]{0,1:T(8,128)(2,1)S(1)} %copy.131), channel_id=1, source_target_pairs={{8,0},{16,8},{24,16},{32,24},{40,32},{48,40},{56,48},{64,56},{72,6... | collective-permute-start | bytes 516104 | tf_op jit(solution)/shard_map/ppermute | solution.py:19
  293.1 52.7 %copy-start.13 = (bf16[224,384]{1,0:T(8,128)(2,1)S(1)}, bf16[224,384]{1,0:T(8,128)(2,1)}, u32[]{:S(2)}) copy-start(bf16[224,384]{1,0:T(8,128)(2,1)} %param.36) | copy-start | bytes 516100
  293.1 52.7 %copy-start.14 = (f32[384]{0:T(512)S(1)}, f32[384]{0:T(512)}, u32[]{:S(2)}) copy-start(f32[384]{0:T(512)} %param.37) | copy-start | bytes 4612
Sparse Core Ops, SparseCore 0:
  9.9 107.1 all-gather.4
  119.7 96.5 all-gather.6
  295.9 48.8 reduce-scatter.3
